TPU v7x, 256 devices: a whole 4x4x8 slice. The times are simulated.
256 devices in a mesh: shot: 16 (over x, y_lo, core), sub: 16 (over y_hi, z).
Axes of the slice: x: 4, y: 4 (y_hi: 2, y_lo: 2; y = y_hi * 2 + y_lo), z: 8, core: 2. Of those that a mesh axis runs over, the one named last changes fastest.
Arguments:
- field_before: float32 [16, 512, 64, 256], P('shot', 'sub'), may hold values from -6 to 6
- field_now: float32 [16, 512, 64, 256], P('shot', 'sub'), may hold values from -6 to 6
- snapshots: bfloat16 [16, 2, 512, 64, 256], P('shot', None, 'sub'), may hold values from -6 to 6
- traces: float32 [16, 16, 2, 128], P('shot', 'sub'), may hold values from -6 to 6
- receivers: int32 [16, 16, 128], P('shot', 'sub'), may hold values from 65536 to 458751, as said below
- courant: float32 [512, 256, 256], P('sub', 'shot'), may hold values from 0.05 to 0.18
- aperture: int32 [16], replicated, may hold values from 0 to 12
- block_of: int32 [16], replicated, may hold values from 0 to 15, each once
Outputs:
- field_prior: float32 [16, 512, 64, 256], P('shot', 'sub')
- field_final: float32 [16, 512, 64, 256], P('shot', 'sub')
- image: float32 [512, 256, 256], P('sub', 'shot')
Inputs may be any that keep to these rules, and one draw needn't show every extreme that they name: `receivers`: each receiver lies at least 4 cells inside its device's part along the first dimension.
All inputs are finite; a program needn't handle non-finite values.
Results may differ from a plain program's by a relative error of at most 0.0003.
Values sent between devices are 32-bit elements; how exact they have to be, the bound alone decides.
A program may use at most 128 MiB of HBM per device.

v0:
```python
import jax
import jax.numpy as jnp
from jax import lax
from jax.sharding import PartitionSpec as P

STEPS = 2


centre_weight = -205.0 / 72.0
side_weights = (8.0 / 5.0, -1.0 / 5.0, 8.0 / 315.0, -1.0 / 560.0)


def with_halo(shard, sides, width):
    for axis, dim in sides:
        size, length = (lax.axis_size(axis), shard.shape[dim])
        up = [(i, (i + 1) % size) for i in range(size - 1)]
        down = [(j, i) for i, j in up]
        last = lax.slice_in_dim(shard, length - width, length, axis=dim)
        first = lax.slice_in_dim(shard, 0, width, axis=dim)
        before = lax.ppermute(last, axis, up)
        after = lax.ppermute(first, axis, down)
        shard = jnp.concatenate([before, shard, after], axis=dim)
    return shard


def laplace(extended):
    size_x = extended.shape[0] - 8
    size_y = extended.shape[1]
    size_z = extended.shape[2]
    padded = jnp.pad(extended, ((0, 0), (4, 4), (4, 4)))

    def window(shift_x, shift_y, shift_z):
        return padded[
            4 + shift_x : 4 + shift_x + size_x,
            4 + shift_y : 4 + shift_y + size_y,
            4 + shift_z : 4 + shift_z + size_z,
        ]

    summed = 3.0 * centre_weight * window(0, 0, 0)
    for distance in range(1, 5):
        weight = side_weights[distance - 1]
        summed = summed + weight * (
            window(distance, 0, 0)
            + window(-distance, 0, 0)
            + window(0, distance, 0)
            + window(0, -distance, 0)
            + window(0, 0, distance)
            + window(0, 0, -distance)
        )
    return summed


def inject(advanced, flat_index, values):
    return advanced.reshape(-1).at[flat_index].add(values).reshape(advanced.shape)


def local(field_before, field_now, snapshots, traces, receivers, courant, aperture, block_of):
    shot_count = block_of.shape[0]
    ranks = jnp.arange(shot_count, dtype=jnp.int32)
    shot_rank = lax.axis_index("shot")
    first_block = jnp.sum(jnp.where(ranks == shot_rank, aperture, 0))
    size_x = field_now.shape[1]
    size_y = field_now.shape[2]
    size_z = field_now.shape[3]
    block_rows = courant.shape[1]
    speed_start = jnp.zeros((size_x, size_y, size_z), jnp.float32)
    block_piece = lax.all_gather(courant, "shot", axis=1, tiled=True)
    row_count = block_piece.shape[1]
    rows = jnp.arange(row_count, dtype=jnp.int32)
    storage = rows // block_rows
    model_block = jnp.sum(
        jnp.where(storage[:, None] == ranks[None, :], block_of[None, :], 0), axis=1
    )
    target = model_block * block_rows + rows % block_rows - first_block * block_rows
    valid = (target >= 0) & (target < size_y)
    target = jnp.where(valid, target, size_y)
    speed = speed_start.at[:, target, :].add(block_piece, mode="drop")
    previous = field_before[0]
    current = field_now[0]
    flat_index = receivers[0, 0]
    shot_traces = traces[0, 0]
    shot_image = jnp.zeros((size_x, size_y, size_z), jnp.float32)
    for instant in range(STEPS):
        extended = with_halo(current, (("sub", 0),), 4)
        advanced = 2.0 * current - previous + speed * laplace(extended)
        advanced = inject(advanced, flat_index, shot_traces[instant])
        shot_image = shot_image + snapshots[0, instant].astype(jnp.float32) * advanced
        previous, current = (current, advanced)
    aperture_rows = jnp.arange(size_y, dtype=jnp.int32)
    model_block = first_block + aperture_rows // block_rows
    storage = jnp.sum(
        jnp.where(block_of[None, :] == model_block[:, None], ranks[None, :], 0), axis=1
    )
    target = storage * block_rows + aperture_rows % block_rows
    spread_terms = (
        jnp.zeros((size_x, shot_count * block_rows, size_z), jnp.float32)
        .at[:, target, :]
        .add(shot_image)
    )
    image = lax.psum_scatter(spread_terms, "shot", scatter_dimension=1, tiled=True)
    return (previous[None], current[None], image)


def solution(mesh):
    in_specs = (
        P("shot", "sub", None, None),
        P("shot", "sub", None, None),
        P("shot", None, "sub", None, None),
        P("shot", "sub", None, None),
        P("shot", "sub", None),
        P("sub", "shot", None),
        P(),
        P(),
    )
    out_specs = (P("shot", "sub", None, None), P("shot", "sub", None, None), P("sub", "shot", None))
    return jax.shard_map(local, mesh=mesh, in_specs=in_specs, out_specs=out_specs, check_vma=False)
```

profile of v0, /device:TPU:1, one launch (start us, length us, event | category | flops | bytes accessed | tf_op | source)
XLA Modules:
  0.0 324.7 jit_solution(8633935603274851507)
XLA Ops:
  8.0 2.8 copy.59
  12.2 5.0 %collective-permute-start.1 = (f32[4,64,256]{2,0,1:T(4,128)S(1)}, f32[4,64,256]{2,0,1:T(4,128)S(1)}, u32[]{:S(2)}, u32[]{:S(2)}) collective-permute-start(f32[4,64,256]{2,0,1:T(4,128)S(1)} %get-tuple-element.17), channel_id=1, source_target_pairs={{0,1},{1,2},{2,3},{3,4},{4,5},{5,6},{6,7},{7,8},{8,9},{9,10},{10,1... | collective-permute-start | bytes 786440 | tf_op jit(solution)/shard_map/ppermute | solution.py:20
  20.5 5.0 %select_maximum_fusion.2 = f32[40,72,264]{2,0,1:T(8,128)} fusion(f32[4,64,256]{2,0,1:T(4,128)S(1)} %collective-permute-done, f32[32,64,256]{2,0,1:T(8,128)S(1)} %bitcast.42, f32[4,64,256]{2,0,1:T(4,128)S(1)} %collective-permute-done.1), kind=kLoop, calls=%fused_computation.19 | loop fusion | flops 11404800 | bytes 5662720 | tf_op jit(solution)/shard_map/concatenate | solution.py:22
  25.5 48.8 %all-gather.2.cloned.1.call-done = f32[32,256,256]{2,1,0:T(8,128)} async-done(((f32[32,16,256]{2,1,0:T(8,128)}), f32[32,256,256]{2,1,0:T(8,128)}) %all-gather.2.cloned.1.call-update) | async-done | bytes 8388624 | tf_op jit(solution)/shard_map/all_gather | solution.py:67
  74.3 11.4 %copy.37 = f32[256,32,256]{2,1,0:T(8,128)} copy(f32[256,32,256]{2,0,1:T(8,128)} %bitcast.44) | data formatting | bytes 16777216 | tf_op jit(solution)/shard_map/all_gather | solution.py:67
  86.0 26.3 %scatter_fusion = f32[32,64,256]{2,0,1:T(8,128)S(1)} fusion(f32[32,64,256]{2,0,1:T(8,128)S(1)} %broadcast_in_dim.46, s32[256]{0:T(256)S(1)} %bitcast.47, f32[256,32,256]{2,1,0:T(8,128)} %copy.37), kind=kCustom, calls=%fused_computation | custom fusion | flops 2097152 | bytes 25166848 | tf_op jit(solution)/shard_map/scatter-add | solution.py:77
  112.3 39.0 %fusion.40 = f32[32,64,256]{2,0,1:T(8,128)S(1)} fusion(f32[32,64,256]{2,0,1:T(8,128)S(1)} %scatter_fusion, f32[32,64,256]{2,0,1:T(8,128)} %bitcast.43, f32[4,64,256]{2,0,1:T(4,128)S(1)} %collective-permute-done.1, f32[4,64,256]{2,0,1:T(4,128)S(1)} %collective-permute-done, f32[40,72,264]{2,0,1:T(8,128)} %select_maximum_fusion.2, f32[1,32,64,256]{3,2,1,0:T(8,128)} %param.8), kind=kLoop, calls=%fused_computation.70 | loop fusion | flops 21495808 | bytes 42467328 | tf_op jit(solution)/shard_map/add | solution.py:85
  152.6 2.4 copy.51
  155.0 4.1 %scatter_fusion.1 = f32[524288]{0:T(1024)} fusion(f32[524288]{0:T(1024)} %bitcast.40, s32[128]{0:T(128)S(1)} %fusion.70, f32[128]{0:T(128)S(1)} %get-tuple-element.21), kind=kCustom, calls=%fused_computation.1 | custom fusion | flops 128 | bytes 2048 | tf_op jit(solution)/shard_map/scatter-add | solution.py:54
  160.2 2.9 reshape.204
  166.2 2.8 constant_dynamic-update-slice_fusion.1
  169.0 5.4 %collective-permute-done.2 = f32[4,64,256]{2,0,1:T(4,128)S(1)} collective-permute-done((f32[4,64,256]{2,0,1:T(4,128)S(1)}, f32[4,64,256]{2,0,1:T(4,128)S(1)}, u32[]{:S(2)}, u32[]{:S(2)}) %collective-permute-start.2) | collective-permute-done | bytes 262176 | tf_op jit(solution)/shard_map/ppermute | solution.py:21
  174.5 3.7 %select_maximum_fusion = f32[40,72,264]{2,0,1:T(8,128)S(1)} fusion(f32[4,64,256]{2,0,1:T(4,128)S(1)} %collective-permute-done.2, f32[32,64,256]{2,0,1:T(8,128)S(1)} %get-tuple-element.13, f32[4,64,256]{2,0,1:T(4,128)S(1)} %collective-permute-done.3), kind=kLoop, calls=%fused_computation.17 | loop fusion | flops 11404800 | bytes 5662720 | tf_op jit(solution)/shard_map/concatenate | solution.py:22
  178.2 13.9 %fusion.13 = f32[32,64,256]{2,0,1:T(8,128)} fusion(f32[32,64,256]{2,0,1:T(8,128)S(1)} %scatter_fusion, f32[32,64,256]{2,0,1:T(8,128)} %copy-done.3, f32[4,64,256]{2,0,1:T(4,128)S(1)} %collective-permute-done.3, f32[40,72,264]{2,0,1:T(8,128)S(1)} %select_maximum_fusion, f32[36,64,256]{2,0,1:T(8,128)S(1)} %constant_dynamic-update-slice_fusion, ...), kind=kLoop, calls=%fused_computation.43 | loop fusion | flops 19398656 | bytes 50593792 | tf_op jit(solution)/shard_map/add | solution.py:85
  192.1 2.8 copy.48
  196.0 2.0 scatter_fusion.2
  198.1 2.0 reshape.206
  200.1 3.4 %fusion.65 = f32[64,32,256]{2,0,1:T(8,128)S(1)} fusion(f32[32,64,256]{2,1,0:T(8,128)} %reshape.206, f32[32,64,256]{2,1,0:T(8,128)} %reshape.204, bf16[1,2,32,64,256]{4,3,2,1,0:T(8,128)(2,1)} %param.10), kind=kLoop, calls=%fused_computation.107 | loop fusion | flops 2621440 | bytes 8388608 | tf_op jit(solution)/shard_map/add | solution.py:87
  204.7 4.3 %broadcast_in_dim.50 = f32[32,256,256]{2,0,1:T(8,128)} broadcast(f32[]{:T(128)} %constant.68.clone.1), dimensions={} | broadcast | bytes 8388612 | tf_op jit(solution)/shard_map/broadcast_in_dim | solution.py:96
  209.0 9.1 %scatter_fusion.3 = f32[32,256,256]{2,0,1:T(8,128)} fusion(f32[32,256,256]{2,0,1:T(8,128)} %broadcast_in_dim.50, s32[64]{0:T(128)S(1)} %fusion.71, f32[64,32,256]{2,1,0:T(8,128)S(1)} %copy.49), kind=kCustom, calls=%fused_computation.3 | custom fusion | flops 524288 | bytes 6291712 | tf_op jit(solution)/shard_map/scatter-add | solution.py:98
  219.6 1.6 broadcast_in_dim_reshape.6
  221.2 2.9 broadcast_in_dim_reshape.7
  224.1 91.7 %reduce-scatter.2.cloned.1.call-done = f32[32,16,256]{2,0,1:T(8,128)} async-done(((f32[32,256,256]{2,0,1:T(8,128)}), f32[32,16,256]{2,0,1:T(8,128)}) %reduce-scatter.2.cloned.1.call-update) | async-done | bytes 524304 | tf_op jit(solution)/shard_map/reduce_scatter | solution.py:100
  315.7 2.1 copy.50
  (47 shorter events, 14.3 us)
Async XLA Ops:
  7.2 67.2 %all-gather.2.cloned.1.call-start = ((), (), s32[]{:S(2)}) async-start(), calls=%async_computation.1 | async-start | bytes 8912896 | tf_op jit(solution)/shard_map/all_gather | solution.py:67
  7.9 9.3 %copy-start.6 = (s32[16]{0:T(128)S(1)}, s32[16]{0:T(128)}, u32[]{:S(2)}) copy-start(s32[16]{0:T(128)} %param.14) | copy-start | bytes 196
  7.9 10.6 %copy-start.5 = (s32[16]{0:T(128)S(1)}, s32[16]{0:T(128)}, u32[]{:S(2)}) copy-start(s32[16]{0:T(128)} %param.15) | copy-start | bytes 196
  7.9 10.8 %copy-start.4 = (f32[1,1,2,128]{3,2,1,0:T(2,128)S(1)}, f32[1,1,2,128]{3,2,1,0:T(2,128)}, u32[]{:S(2)}) copy-start(f32[1,1,2,128]{3,2,1,0:T(2,128)} %param.11) | copy-start | bytes 3076
  7.9 10.8 %copy-start.7 = (s32[1,1,128]{2,1,0:T(1,128)S(1)}, s32[1,1,128]{2,1,0:T(1,128)}, u32[]{:S(2)}) copy-start(s32[1,1,128]{2,1,0:T(1,128)} %param.12) | copy-start | bytes 1540
  7.9 307.8 %reduce-scatter.2.cloned.1.call-start = ((), (), s32[]{:S(2)}) async-start(), calls=%async_computation.2 | async-start | bytes 8912896 | tf_op jit(solution)/shard_map/reduce_scatter | solution.py:100
  10.8 14.7 %copy-start.2 = (f32[1,32,64,256]{3,1,2,0:T(8,128)}, f32[1,32,64,256]{3,1,2,0:T(8,128)S(1)}, u32[]{:S(2)}) copy-start(f32[1,32,64,256]{3,1,2,0:T(8,128)S(1)} %copy.59) | copy-start | bytes 6291460
  10.9 8.5 %collective-permute-start = (f32[4,64,256]{2,0,1:T(4,128)S(1)}, f32[4,64,256]{2,0,1:T(4,128)S(1)}, u32[]{:S(2)}, u32[]{:S(2)}) collective-permute-start(f32[4,64,256]{2,0,1:T(4,128)S(1)} %get-tuple-element.16), channel_id=1, source_target_pairs={{1,0},{2,1},{3,2},{4,3},{5,4},{6,5},{7,6},{8,7},{9,8},{10,9},{11,1... | collective-permute-start | bytes 786440 | tf_op jit(solution)/shard_map/ppermute | solution.py:21
  12.2 8.3 %collective-permute-start.1 = (f32[4,64,256]{2,0,1:T(4,128)S(1)}, f32[4,64,256]{2,0,1:T(4,128)S(1)}, u32[]{:S(2)}, u32[]{:S(2)}) collective-permute-start(f32[4,64,256]{2,0,1:T(4,128)S(1)} %get-tuple-element.17), channel_id=1, source_target_pairs={{0,1},{1,2},{2,3},{3,4},{4,5},{5,6},{6,7},{7,8},{8,9},{9,10},{10,1... | collective-permute-start | bytes 786440 | tf_op jit(solution)/shard_map/ppermute | solution.py:20
  163.6 10.9 %collective-permute-start.3 = (f32[4,64,256]{2,0,1:T(4,128)S(1)}, f32[4,64,256]{2,0,1:T(4,128)S(1)}, u32[]{:S(2)}, u32[]{:S(2)}) collective-permute-start(f32[4,64,256]{2,0,1:T(4,128)S(1)} %copy.45), channel_id=1, source_target_pairs={{0,1},{1,2},{2,3},{3,4},{4,5},{5,6},{6,7},{7,8},{8,9},{9,10},{10,1... | collective-permute-start | bytes 786440 | tf_op jit(solution)/shard_map/ppermute | solution.py:20
  164.9 9.5 %collective-permute-start.2 = (f32[4,64,256]{2,0,1:T(4,128)S(1)}, f32[4,64,256]{2,0,1:T(4,128)S(1)}, u32[]{:S(2)}, u32[]{:S(2)}) collective-permute-start(f32[4,64,256]{2,0,1:T(4,128)S(1)} %copy.43), channel_id=1, source_target_pairs={{1,0},{2,1},{3,2},{4,3},{5,4},{6,5},{7,6},{8,7},{9,8},{10,9},{11,1... | collective-permute-start | bytes 786440 | tf_op jit(solution)/shard_map/ppermute | solution.py:21
  169.0 5.5 %copy-start.3 = (f32[32,64,256]{2,0,1:T(8,128)}, f32[32,64,256]{2,0,1:T(8,128)S(1)}, u32[]{:S(2)}) copy-start(f32[32,64,256]{2,0,1:T(8,128)S(1)} %get-tuple-element.13) | copy-start | bytes 6291460
  198.1 2.0 copy-start.1
  218.0 1.6 copy-start
Sparse Core Ops, SparseCore 0:
  9.8 64.4 all-gather.1
  218.2 97.5 reduce-scatter.1
where the time goes:
time: 326 us; the launch traced here: 325 us
  waiting for transfers between devices  148 us (45%)
  other arithmetic  108 us (33%)
  local copies, waits for them, and re-layouts  45.1 us (14%)
  between operations  15 us (5%)
  starting transfers between devices  8.98 us (3%)
    reduce_scatter x1, waiting for transfers between devices, local(): lax.psum_scatter(spread_terms, 'shot', scatter_dimension=1, tiled=True)  91.7 us
    add x2, other arithmetic, local(): advanced = 2.0 * current - previous + speed * laplace(extended)  53 us
    all_gather x1, waiting for transfers between devices, local(): block_piece = lax.all_gather(courant, 'shot', axis=1, tiled=True)  48.8 us
    scatter-add x1, other arithmetic, local(): speed = speed_start.at[:, target, :].add(block_piece, mode='drop')  26.3 us
    unnamed x21, local copies, waits for them, and re-layouts  12.8 us
    all_gather x1, local copies, waits for them, and re-layouts, local(): block_piece = lax.all_gather(courant, 'shot', axis=1, tiled=True)  11.4 us
    scatter-add x1, other arithmetic, local(): spread_terms = jnp.zeros((size_x, shot_count * block_rows, size_z), jnp.f...  9.05 us
    concatenate x2, other arithmetic, with_halo(): shard = jnp.concatenate([before, shard, after], axis=dim)  8.66 us
  transfers between devices with their start and end apart: 6, of which 4 were waited for; matrix products, arithmetic and copies ran while one was open for 5% of the time, Pallas kernels for 0%

commit v1 on v0

v1 whole, which is shorter than its diff:
```python
import functools

import jax
import jax.numpy as jnp
import ml_dtypes
import numpy as np
from jax import lax
from jax.experimental import pallas as pl
from jax.experimental.pallas import tpu as pltpu
from jax.sharding import PartitionSpec as P

MESH = pl.DeviceIdType.MESH
F32 = jnp.float32
BF16 = jnp.bfloat16

NX, NY, NZ, BY, NB, NR = 32, 64, 256, 16, 16, 128
HALO = 4
centre_weight = -205.0 / 72.0
side_weights = (8.0 / 5.0, -1.0 / 5.0, 8.0 / 315.0, -1.0 / 560.0)

CHUNKS = ((0, 8, 2), (8, 8, 3), (16, 8, 3), (24, 8, 2))
ORDER = (0, 3, 1, 2)
OWN, A, B, D = range(4)


def split(value):
    high = value.astype(BF16)
    low = (value - high.astype(F32)).astype(BF16)
    return high, low


def band(i, j):
    apart = jnp.abs(i - j)
    high = jnp.zeros(apart.shape, F32)
    low = jnp.zeros(apart.shape, F32)
    for distance in range(1, 5):
        weight = np.float32(side_weights[distance - 1])
        top = np.float32(weight.astype(ml_dtypes.bfloat16))
        high = jnp.where(apart == distance, float(top), high)
        low = jnp.where(apart == distance, float(weight - top), low)
    return high.astype(BF16), low.astype(BF16)


def kernel(before, now, snapshots, traces, receivers, courant, aperture, block_of,
           prior_out, final_out, image_out,
           fpad, npad, base, lap, last, snap, wz, wy, spots,
           speed, gath, stage, img, imgin, sibout, sibin, acc, xin, yin, imgout,
           send_sems, recv_sems, local_sems):
    s = lax.axis_index("shot")
    u = lax.axis_index("sub")
    c = lax.rem(s, 2)
    y = lax.rem(s // 2, 2)
    x = s // 4
    way = 1 - 2 * c

    def at(x_, y_, c_):
        return {"shot": (x_ * 2 + y_) * 2 + c_, "sub": u}

    def column(role, way_):
        return lax.rem({OWN: x, A: x - way_ + 4, B: x + way_ + 4, D: x + 2}[role], 4)

    dev = {
        "A": at(column(A, way), y, c),
        "B": at(column(B, way), y, c),
        "Y": at(x, 1 - y, c),
        "C": at(x, y, 1 - c),
        "S+": {"shot": s, "sub": lax.rem(u + 1, 16)},
        "S-": {"shot": s, "sub": lax.rem(u + 15, 16)},
    }
    ids = {}
    sent = []

    def number(name):
        return ids.setdefault(name, len(ids))

    def copy_of(name, src, dst, to):
        n = number(name)
        return pltpu.make_async_remote_copy(
            src_ref=src, dst_ref=dst, send_sem=send_sems.at[n], recv_sem=recv_sems.at[n],
            device_id=dev[to], device_id_type=MESH)

    def send(name, src, dst, to):
        copy = copy_of(name, src, dst, to)
        copy.start()
        sent.append(copy)

    def arrive(name, dst):
        copy_of(name, dst, dst, "Y").wait_recv()

    locals_ = {}

    def local(name, src, dst):
        copy = pltpu.make_async_copy(src, dst, local_sems.at[len(locals_)])
        locals_[name] = copy
        copy.start()

    def shape_of(k):
        first, size, h = CHUNKS[k]
        return first, size, h, size - h

    for k in ORDER:
        first, size, h, r = shape_of(k)
        local(("own", k), courant.at[pl.ds(first + y * h, r)], gath[k].at[c * 8 + x * 2 + y])
    for k in (1, 2, 0, 3):
        first, size, h, r = shape_of(k)
        local(("now", k), now.at[0, pl.ds(first, size)], fpad.at[pl.ds(HALO + first, size)])
    for k in (1, 2, 0, 3):
        first, size, h, r = shape_of(k)
        local(("before", k), before.at[0, pl.ds(first, size)], base.at[pl.ds(first, size)])
    local("snap", snapshots.at[0], snap)

    barrier = pltpu.get_barrier_semaphore()
    for name in dev:
        pl.semaphore_signal(barrier, inc=1, device_id=dev[name], device_id_type=MESH)
    pl.semaphore_wait(barrier, len(dev))

    def halo_send(name, up_src, down_src, pad):
        up = copy_of(name + "up", up_src, pad.at[pl.ds(0, HALO)], "S+")
        down = copy_of(name + "down", down_src, pad.at[pl.ds(HALO + NX, HALO)], "S-")

        @pl.when(u < 15)
        def _():
            up.start()

        @pl.when(u > 0)
        def _():
            down.start()

        return up, down

    def halo_low(copies):
        @pl.when(u > 0)
        def _():
            copies[0].wait_recv()

    def halo_high(copies):
        @pl.when(u < 15)
        def _():
            copies[1].wait_recv()

    def halo_sent(copies):
        @pl.when(u < 15)
        def _():
            copies[0].wait_send()

        @pl.when(u > 0)
        def _():
            copies[1].wait_send()

    def pair(role, c_):
        return pl.ds(c_ * 8 + 2 * column(role, 1 - 2 * c_), 2)

    def gather_y(k):
        first, size, h, r = shape_of(k)
        send(("gy", k), courant.at[pl.ds(first + (1 - y) * h, r)], gath[k].at[c * 8 + x * 2 + y], "Y")

    def gather_x(k):
        arrive(("gy", k), gath[k].at[c * 8 + x * 2 + 1 - y])
        locals_[("own", k)].wait()
        mine = gath[k].at[pair(OWN, c)]
        send(("ga", k), mine, mine, "A")
        send(("gb", k), mine, mine, "B")
        send(("gc", OWN, k), mine, mine, "C")

    def gather_forward(k):
        from_a = gath[k].at[pair(A, c)]
        arrive(("gb", k), from_a)
        send(("gd", k), from_a, from_a, "B")
        send(("gc", A, k), from_a, from_a, "C")

    def gather_sibling(k):
        from_b = gath[k].at[pair(B, c)]
        arrive(("ga", k), from_b)
        send(("gc", B, k), from_b, from_b, "C")
        from_d = gath[k].at[pair(D, c)]
        arrive(("gd", k), from_d)
        send(("gc", D, k), from_d, from_d, "C")

    def slots_from(first_block):
        found = []
        for j in range(4):
            slot = 0
            for b in range(NB):
                slot = jnp.where(block_of[b] == first_block + j, (b % 2) * 8 + b // 2, slot)
            found.append(slot)
        return found

    def gather_stage(k):
        first, size, h, r = shape_of(k)
        for role in (OWN, A, B, D):
            arrive(("gc", role, k), gath[k].at[pair(role, 1 - c)])
        for j in range(4):
            stage[k][:, BY * j:BY * j + BY, :] = gath[k][their_slots[j], pl.ds(y * (r - h), h)]
        send(("gs", k), stage[k], speed[k].at[pl.ds(y * r, h)], "Y")
        for j in range(4):
            speed[k][pl.ds(y * h, r), BY * j:BY * j + BY, :] = gath[k][my_slots[j]]

    def matrices():
        i = lax.broadcasted_iota(jnp.int32, (256, 256), 0)
        j = lax.broadcasted_iota(jnp.int32, (256, 256), 1)
        high, low = band(i, j)
        wz[0:256, :] = high
        wz[256:512, :] = high
        wz[512:768, :] = low
        same = (i // NY) == (j // NY)
        high = jnp.where(same, high.astype(F32), 0.0).astype(BF16)
        low = jnp.where(same, low.astype(F32), 0.0).astype(BF16)
        wy[:, 0:256] = high
        wy[:, 256:512] = high
        wy[:, 512:768] = low

    def depth_spots():
        z = lax.broadcasted_iota(jnp.int32, (NZ, NR), 0)
        at_depth = z == lax.rem(receivers[0], NZ)
        for t in range(2):
            value = jnp.where(at_depth, traces[0, 0, t:t + 1, :], 0.0)
            high = value.astype(BF16)
            rest = value - high.astype(F32)
            middle = rest.astype(BF16)
            low = (rest - middle.astype(F32)).astype(BF16)
            spots[t, :, 0:NR] = high
            spots[t, :, NR:2 * NR] = middle
            spots[t, :, 2 * NR:3 * NR] = low

    def injected(layer, t):
        row = lax.broadcasted_iota(jnp.int32, (4 * NY, NR), 0) + layer * NY
        hit = jnp.where(row == receivers[0] // NZ, 1.0, 0.0).astype(BF16)
        hits = jnp.concatenate([hit, hit, hit], axis=1)
        return lax.dot_general(hits, spots[t], (((1,), (1,)), ((), ())), preferred_element_type=F32)

    def laplace(pad, layer):
        field = pad[pl.ds(layer + HALO, 4)]
        rows = field.reshape(4 * NY, NZ)
        high, low = split(rows)
        summed = jnp.dot(jnp.concatenate([high, low, high], axis=1), wz[...], preferred_element_type=F32)
        summed = summed + jnp.dot(wy[...], jnp.concatenate([high, low, high], axis=0), preferred_element_type=F32)
        summed = summed.reshape(4, NY, NZ) + (3.0 * centre_weight) * field
        for distance in range(1, 5):
            summed = summed + side_weights[distance - 1] * (
                pad[pl.ds(layer + HALO + distance, 4)] + pad[pl.ds(layer + HALO - distance, 4)])
        return field, summed

    def groups(k, body):
        first, size, h, r = shape_of(k)

        def step(g, carry):
            body(first + 4 * g, 4 * g)
            return carry

        lax.fori_loop(0, size // 4, step, 0)

    def prepare(k):
        locals_[("before", k)].wait()

        def body(layer, inside):
            field, summed = laplace(fpad, layer)
            lap[pl.ds(layer, 4)] = summed
            base[pl.ds(layer, 4)] = (2.0 * field - base[pl.ds(layer, 4)]
                                     + injected(layer, 0).reshape(4, NY, NZ))

        groups(k, body)

    def step_one(k):
        first, size, h, r = shape_of(k)
        arrive(("gs", k), speed[k].at[pl.ds((1 - y) * r, h)])

        def body(layer, inside):
            npad[pl.ds(layer + HALO, 4)] = (base[pl.ds(layer, 4)]
                                            + speed[k][pl.ds(inside, 4)] * lap[pl.ds(layer, 4)])

        groups(k, body)
        local(("prior", k), npad.at[pl.ds(HALO + first, size)], prior_out.at[0, pl.ds(first, size)])

    def step_two(k):
        first, size, h, r = shape_of(k)

        def body(layer, inside):
            field, summed = laplace(npad, layer)
            value = (2.0 * field - fpad[pl.ds(layer + HALO, 4)] + speed[k][pl.ds(inside, 4)] * summed
                     + injected(layer, 1).reshape(4, NY, NZ))
            last[pl.ds(layer, 4)] = value
            seen = snap[0, pl.ds(layer, 4)].astype(F32) * field + snap[1, pl.ds(layer, 4)].astype(F32) * value
            for j in range(4):
                img[k][j, pl.ds(inside, 4)] = seen[:, BY * j:BY * j + BY, :]

        groups(k, body)
        local(("final", k), last.at[pl.ds(first, size)], final_out.at[0, pl.ds(first, size)])
        img[k][4] = jnp.zeros((size, BY, NZ), F32)
        imgin[k][4] = jnp.zeros((h, BY, NZ), F32)
        send(("ry", k), img[k].at[pl.ds(0, 4), pl.ds((1 - y) * r, h)], imgin[k].at[pl.ds(0, 4)], "Y")

    def place(first_block, storage):
        block = block_of[storage] - first_block
        return jnp.where((block >= 0) & (block < 4), block, 4)

    def reduce_sibling(k):
        first, size, h, r = shape_of(k)
        arrive(("ry", k), imgin[k].at[pl.ds(0, 4)])
        for to, core in ((sibout[k], 1 - c), (acc[k], c)):
            def body(slot, carry, to=to, core=core):
                storage = 2 * slot + core
                to[slot] = img[k][place(my_first, storage), pl.ds(y * h, r)]
                inner = pl.ds(y * (r - h), h)
                to[slot, inner] = to[slot, inner] + imgin[k][place(their_first, storage)]
                return carry

            lax.fori_loop(0, 8, body, 0)
            if to is sibout[k]:
                send(("rc", k), sibout[k], sibin[k], "C")

    def reduce_x(k):
        arrive(("rc", k), sibin[k])

        def body(slot, carry):
            acc[k][slot] = acc[k][slot] + sibin[k][slot]
            return carry

        lax.fori_loop(0, 8, body, 0)
        send(("rd", k), acc[k].at[pl.ds(2 * column(D, way), 2)], xin[k].at[0], "B")
        send(("ra", k), acc[k].at[pl.ds(2 * column(A, way), 2)], xin[k].at[1], "A")

    def reduce_forward(k):
        arrive(("rd", k), xin[k].at[0])
        to_b = pl.ds(2 * column(B, way), 2)
        acc[k][to_b] = acc[k][to_b] + xin[k][0]
        send(("rb", k), acc[k].at[to_b], xin[k].at[2], "B")

    def reduce_y(k):
        arrive(("ra", k), xin[k].at[1])
        arrive(("rb", k), xin[k].at[2])
        mine = pl.ds(2 * x, 2)
        acc[k][mine] = acc[k][mine] + xin[k][1] + xin[k][2]
        send(("rz", k), acc[k].at[2 * x + 1 - y], yin[k], "Y")

    def finish(k):
        first, size, h, r = shape_of(k)
        arrive(("rz", k), yin[k])
        imgout[k][...] = jnp.zeros((size, BY, NZ), F32)
        imgout[k][pl.ds(y * h, r)] = acc[k][2 * x + y]
        theirs = pl.ds((1 - y) * h, r)
        imgout[k][theirs] = imgout[k][theirs] + yin[k][...]
        local(("image", k), imgout[k], image_out.at[pl.ds(first, size)])

    for k in ORDER:
        gather_y(k)
    first_halo = halo_send("h0", now.at[0, pl.ds(NX - HALO, HALO)], now.at[0, pl.ds(0, HALO)], fpad)

    @pl.when(u == 0)
    def _():
        fpad[0:HALO] = jnp.zeros((HALO, NY, NZ), F32)
        npad[0:HALO] = jnp.zeros((HALO, NY, NZ), F32)

    @pl.when(u == 15)
    def _():
        fpad[HALO + NX:] = jnp.zeros((HALO, NY, NZ), F32)
        npad[HALO + NX:] = jnp.zeros((HALO, NY, NZ), F32)

    my_first = aperture[s]
    their_first = aperture[(x * 2 + 1 - y) * 2 + c]
    my_slots = slots_from(my_first)
    their_slots = slots_from(their_first)
    matrices()
    depth_spots()
    gather_x(0)
    gather_x(3)
    for k in (1, 2, 0, 3):
        locals_[("now", k)].wait()
    prepare(1)
    gather_forward(0)
    gather_x(1)
    prepare(2)
    gather_sibling(0)
    gather_forward(3)
    gather_x(2)
    halo_low(first_halo)
    prepare(0)
    gather_stage(0)
    halo_high(first_halo)
    prepare(3)
    gather_sibling(3)
    gather_forward(1)
    gather_stage(3)
    step_one(0)
    gather_sibling(1)
    gather_forward(2)
    gather_stage(1)
    step_one(3)
    second_halo = halo_send("h1", npad.at[pl.ds(NX, HALO)], npad.at[pl.ds(HALO, HALO)], npad)
    locals_["snap"].wait()
    gather_sibling(2)
    gather_stage(2)
    step_one(1)
    halo_low(second_halo)
    step_two(0)
    step_one(2)
    halo_high(second_halo)
    step_two(3)
    reduce_sibling(0)
    step_two(1)
    reduce_x(0)
    reduce_sibling(3)
    step_two(2)
    reduce_forward(0)
    reduce_x(3)
    reduce_sibling(1)
    reduce_y(0)
    reduce_forward(3)
    reduce_x(1)
    reduce_sibling(2)
    finish(0)
    reduce_y(3)
    reduce_forward(1)
    reduce_x(2)
    finish(3)
    reduce_y(1)
    reduce_forward(2)
    finish(1)
    reduce_y(2)
    finish(2)

    halo_sent(first_halo)
    halo_sent(second_halo)
    for copy in sent:
        copy.wait_send()
    for name in locals_:
        if name[0] in ("prior", "final", "image"):
            locals_[name].wait()


def local(field_before, field_now, snapshots, traces, receivers, courant, aperture, block_of):
    anywhere = pl.BlockSpec(memory_space=pl.ANY)
    vector = pl.BlockSpec(memory_space=pltpu.VMEM)
    scalar = pl.BlockSpec(memory_space=pltpu.SMEM)

    def per_chunk(dims):
        return [pltpu.VMEM(dims(size, h, size - h), F32) for first, size, h in CHUNKS]

    field = (NX, NY, NZ)
    padded = (NX + 2 * HALO, NY, NZ)
    block = (BY, NZ)
    count = 16 * len(CHUNKS) + 8
    scratch = [
        pltpu.VMEM(padded, F32), pltpu.VMEM(padded, F32),
        pltpu.VMEM(field, F32), pltpu.VMEM(field, F32), pltpu.VMEM(field, F32),
        pltpu.VMEM((2,) + field, BF16),
        pltpu.VMEM((768, 256), BF16), pltpu.VMEM((256, 768), BF16),
        pltpu.VMEM((2, NZ, 3 * NR), BF16),
        per_chunk(lambda n, h, r: (n, NY, NZ)),
        per_chunk(lambda n, h, r: (NB, r) + block),
        per_chunk(lambda n, h, r: (h, NY, NZ)),
        per_chunk(lambda n, h, r: (5, n) + block),
        per_chunk(lambda n, h, r: (5, h) + block),
        per_chunk(lambda n, h, r: (8, r) + block),
        per_chunk(lambda n, h, r: (8, r) + block),
        per_chunk(lambda n, h, r: (8, r) + block),
        per_chunk(lambda n, h, r: (3, 2, r) + block),
        per_chunk(lambda n, h, r: (r,) + block),
        per_chunk(lambda n, h, r: (n,) + block),
        pltpu.SemaphoreType.DMA((count,)),
        pltpu.SemaphoreType.DMA((count,)),
        pltpu.SemaphoreType.DMA((8 * len(CHUNKS),)),
    ]
    return pl.pallas_call(
        kernel,
        out_shape=(
            jax.ShapeDtypeStruct(field_now.shape, F32),
            jax.ShapeDtypeStruct(field_now.shape, F32),
            jax.ShapeDtypeStruct(courant.shape, F32),
        ),
        in_specs=[anywhere, anywhere, anywhere, vector, vector, anywhere, scalar, scalar],
        out_specs=(anywhere, anywhere, anywhere),
        scratch_shapes=scratch,
        compiler_params=pltpu.CompilerParams(
            collective_id=0, has_side_effects=True, vmem_limit_bytes=60 << 20),
    )(field_before, field_now, snapshots, traces, receivers, courant, aperture, block_of)


def solution(mesh):
    in_specs = (
        P("shot", "sub", None, None),
        P("shot", "sub", None, None),
        P("shot", None, "sub", None, None),
        P("shot", "sub", None, None),
        P("shot", "sub", None),
        P("sub", "shot", None),
        P(),
        P(),
    )
    out_specs = (P("shot", "sub", None, None), P("shot", "sub", None, None), P("sub", "shot", None))
    return jax.shard_map(local, mesh=mesh, in_specs=in_specs, out_specs=out_specs, check_vma=False)
```

time: 326 us -> 110 us (0.34)
  the two profiles are of different devices: /device:TPU:1 before, /device:TPU:32 now
where the time goes in v1:
time: 110 us
  Pallas kernels  104 us (95%)
  local copies, waits for them, and re-layouts  5.47 us (5%)
    pallas_call x1, Pallas kernels, local(): pl.pallas_call(kernel, out_shape=(jax.ShapeDtypeStruct(field_now.shape, F...  104 us
    unnamed x7, local copies, waits for them, and re-layouts  5.47 us

profile of v1, /device:TPU:32, one launch (start us, length us, event | category | flops | bytes accessed | tf_op | source)
XLA Modules:
  0.0 109.7 jit_solution(2933326172318014174)
XLA Ops:
  0.6 103.6 %shard_map.103 = (f32[1,32,64,256]{3,2,1,0:T(8,128)}, f32[1,32,64,256]{3,2,1,0:T(8,128)}, f32[32,16,256]{2,1,0:T(8,128)}) custom-call(f32[1,32,64,256]{3,2,1,0:T(8,128)} %before.1, f32[1,32,64,256]{3,2,1,0:T(8,128)} %now.1, bf16[1,2,32,64,256]{4,3,2,1,0:T(8,128)(2,1)} %snapshots.1, f32[1,1,2,128]{3,2,1,0:T(2,128)} %traces.1, s32[1,1,128]{2,1,0:T(1,128)} %receivers.1, ...), custom_call_target="tpu_custom_call" | custom-call | tf_op jit(solution)/shard_map/pallas_call | solution.py:463
  104.2 0.0 copy-start
  104.2 3.3 %copy.14 = f32[1,32,64,256]{3,2,1,0:T(8,128)} copy(f32[1,32,64,256]{3,2,1,0:T(8,128)} %get-tuple-element.6) | data formatting | bytes 4194304
  107.5 0.0 copy-done
  107.5 0.0 copy-start.1
  107.5 1.3 %copy.15 = f32[1,32,64,256]{3,2,1,0:T(8,128)} copy(f32[1,32,64,256]{3,2,1,0:T(8,128)S(1)} %copy-done) | data formatting | bytes 4194304
  108.9 0.1 copy-done.1
  108.9 0.8 copy.16
Async XLA Ops:
  104.2 3.3 %copy-start = (f32[1,32,64,256]{3,2,1,0:T(8,128)S(1)}, f32[1,32,64,256]{3,2,1,0:T(8,128)}, u32[]{:S(2)}) copy-start(f32[1,32,64,256]{3,2,1,0:T(8,128)} %get-tuple-element.7) | copy-start | bytes 6291460
  107.5 1.4 %copy-start.1 = (f32[32,16,256]{2,1,0:T(8,128)S(1)}, f32[32,16,256]{2,1,0:T(8,128)}, u32[]{:S(2)}) copy-start(f32[32,16,256]{2,1,0:T(8,128)} %get-tuple-element.8) | copy-start | bytes 1572868

commit v2 on v1

--- a/solution.py
+++ b/solution.py
@@ -18,8 +18,20 @@
 centre_weight = -205.0 / 72.0
 side_weights = (8.0 / 5.0, -1.0 / 5.0, 8.0 / 315.0, -1.0 / 560.0)
 
-CHUNKS = ((0, 8, 2), (8, 8, 3), (16, 8, 3), (24, 8, 2))
-ORDER = (0, 3, 1, 2)
+CHUNKS = ((0, 4, 1), (4, 4, 2), (8, 4, 2), (12, 4, 2), (16, 4, 2), (20, 4, 1), (24, 4, 0), (28, 4, 0))
+ORDER = (0, 7, 1, 2, 3, 4, 5, 6)
+LOADS = tuple(range(1, len(CHUNKS) - 1)) + (0, len(CHUNKS) - 1)
+SEQUENCE = (
+    "o4", "o1", "o0", "o2", "x0", "o7", "x7", "M0", "P4", "x1", "x4", "b0", "a0", "o5",
+    "x5", "b1", "P6", "a7", "a4", "P5", "P2", "x2", "b7", "a1", "o6", "x6", "d0", "b4",
+    "a5", "d7", "s0", "d4", "P7", "o3", "x3", "s4", "d1", "P0", "a2", "b5", "b2", "s7",
+    "17", "b6", "10", "H0", "P1", "s1", "a6", "d5", "a3", "b3", "s5", "d2", "s2", "d6",
+    "P3", "d3", "14", "s3", "s6", "16", "15", "26", "p6", "11", "20", "27", "p7", "25",
+    "12", "q6", "13", "23", "q7", "24", "r6", "p0", "22", "p5", "21", "q0", "q5", "p3",
+    "q3", "t6", "p4", "r0", "r7", "r5", "p2", "r3", "q4", "R5", "q2", "p1", "q1", "t3",
+    "t0", "t7", "r2", "R3", "r4", "t5", "R0", "r1", "R1", "R6", "t2", "R7", "R2", "t4",
+    "R4", "t1", "f3", "f5", "f7", "f0", "f6", "f4", "f2", "f1",
+)
 OWN, A, B, D = range(4)
 
 
@@ -67,6 +79,10 @@
         "S+": {"shot": s, "sub": lax.rem(u + 1, 16)},
         "S-": {"shot": s, "sub": lax.rem(u + 15, 16)},
     }
+    barrier = pltpu.get_barrier_semaphore()
+    for name in dev:
+        pl.semaphore_signal(barrier, inc=1, device_id=dev[name], device_id_type=MESH)
+    first_two = [int(name[1:]) for name in SEQUENCE if name[0] == "2"][0]
     ids = {}
     sent = []
 
@@ -101,17 +117,14 @@
     for k in ORDER:
         first, size, h, r = shape_of(k)
         local(("own", k), courant.at[pl.ds(first + y * h, r)], gath[k].at[c * 8 + x * 2 + y])
-    for k in (1, 2, 0, 3):
+    for k in LOADS:
         first, size, h, r = shape_of(k)
         local(("now", k), now.at[0, pl.ds(first, size)], fpad.at[pl.ds(HALO + first, size)])
-    for k in (1, 2, 0, 3):
+    for k in LOADS:
         first, size, h, r = shape_of(k)
         local(("before", k), before.at[0, pl.ds(first, size)], base.at[pl.ds(first, size)])
     local("snap", snapshots.at[0], snap)
 
-    barrier = pltpu.get_barrier_semaphore()
-    for name in dev:
-        pl.semaphore_signal(barrier, inc=1, device_id=dev[name], device_id_type=MESH)
     pl.semaphore_wait(barrier, len(dev))
 
     def halo_send(name, up_src, down_src, pad):
@@ -154,27 +167,39 @@
         first, size, h, r = shape_of(k)
         send(("gy", k), courant.at[pl.ds(first + (1 - y) * h, r)], gath[k].at[c * 8 + x * 2 + y], "Y")
 
+    def gather_own(k):
+        locals_[("own", k)].wait()
+        mine = gath[k].at[c * 8 + x * 2 + y]
+        send(("ga", 0, k), mine, mine, "A")
+        send(("gb", 0, k), mine, mine, "B")
+
     def gather_x(k):
-        arrive(("gy", k), gath[k].at[c * 8 + x * 2 + 1 - y])
-        locals_[("own", k)].wait()
-        mine = gath[k].at[pair(OWN, c)]
-        send(("ga", k), mine, mine, "A")
-        send(("gb", k), mine, mine, "B")
-        send(("gc", OWN, k), mine, mine, "C")
-
-    def gather_forward(k):
-        from_a = gath[k].at[pair(A, c)]
-        arrive(("gb", k), from_a)
-        send(("gd", k), from_a, from_a, "B")
-        send(("gc", A, k), from_a, from_a, "C")
-
-    def gather_sibling(k):
-        from_b = gath[k].at[pair(B, c)]
-        arrive(("ga", k), from_b)
-        send(("gc", B, k), from_b, from_b, "C")
-        from_d = gath[k].at[pair(D, c)]
-        arrive(("gd", k), from_d)
-        send(("gc", D, k), from_d, from_d, "C")
+        theirs = gath[k].at[c * 8 + x * 2 + 1 - y]
+        arrive(("gy", k), theirs)
+        send(("ga", 1, k), theirs, theirs, "A")
+        send(("gb", 1, k), theirs, theirs, "B")
+        both = gath[k].at[pair(OWN, c)]
+        send(("gc", OWN, k), both, both, "C")
+
+    def gather_a(k):
+        column_a = column(A, way)
+        arrive(("gb", 0, k), gath[k].at[c * 8 + 2 * column_a + y])
+        arrive(("gb", 1, k), gath[k].at[c * 8 + 2 * column_a + 1 - y])
+        both = gath[k].at[pair(A, c)]
+        send(("gd", k), both, both, "B")
+        send(("gc", A, k), both, both, "C")
+
+    def gather_b(k):
+        column_b = column(B, way)
+        arrive(("ga", 0, k), gath[k].at[c * 8 + 2 * column_b + y])
+        arrive(("ga", 1, k), gath[k].at[c * 8 + 2 * column_b + 1 - y])
+        both = gath[k].at[pair(B, c)]
+        send(("gc", B, k), both, both, "C")
+
+    def gather_d(k):
+        both = gath[k].at[pair(D, c)]
+        arrive(("gd", k), both)
+        send(("gc", D, k), both, both, "C")
 
     def slots_from(first_block):
         found = []
@@ -189,9 +214,10 @@
         first, size, h, r = shape_of(k)
         for role in (OWN, A, B, D):
             arrive(("gc", role, k), gath[k].at[pair(role, 1 - c)])
-        for j in range(4):
+        for j in range(4 if h else 0):
             stage[k][:, BY * j:BY * j + BY, :] = gath[k][their_slots[j], pl.ds(y * (r - h), h)]
-        send(("gs", k), stage[k], speed[k].at[pl.ds(y * r, h)], "Y")
+        if h:
+            send(("gs", k), stage[k], speed[k].at[pl.ds(y * r, h)], "Y")
         for j in range(4):
             speed[k][pl.ds(y * h, r), BY * j:BY * j + BY, :] = gath[k][my_slots[j]]
 
@@ -243,6 +269,10 @@
     def groups(k, body):
         first, size, h, r = shape_of(k)
 
+        if size == 4:
+            body(first, 0)
+            return
+
         def step(g, carry):
             body(first + 4 * g, 4 * g)
             return carry
@@ -250,6 +280,10 @@
         lax.fori_loop(0, size // 4, step, 0)
 
     def prepare(k):
+        if k == 0:
+            halo_low(first_halo)
+        if k == len(CHUNKS) - 1:
+            halo_high(first_halo)
         locals_[("before", k)].wait()
 
         def body(layer, inside):
@@ -260,9 +294,14 @@
 
         groups(k, body)
 
+    def gather_end(k):
+        first, size, h, r = shape_of(k)
+        if h:
+            arrive(("gs", k), speed[k].at[pl.ds((1 - y) * r, h)])
+
     def step_one(k):
         first, size, h, r = shape_of(k)
-        arrive(("gs", k), speed[k].at[pl.ds((1 - y) * r, h)])
+        gather_end(k)
 
         def body(layer, inside):
             npad[pl.ds(layer + HALO, 4)] = (base[pl.ds(layer, 4)]
@@ -273,6 +312,12 @@
 
     def step_two(k):
         first, size, h, r = shape_of(k)
+        if k == 0:
+            halo_low(second_halo)
+        if k == len(CHUNKS) - 1:
+            halo_high(second_halo)
+        if k == first_two:
+            locals_["snap"].wait()
 
         def body(layer, inside):
             field, summed = laplace(npad, layer)
@@ -286,8 +331,9 @@
         groups(k, body)
         local(("final", k), last.at[pl.ds(first, size)], final_out.at[0, pl.ds(first, size)])
         img[k][4] = jnp.zeros((size, BY, NZ), F32)
-        imgin[k][4] = jnp.zeros((h, BY, NZ), F32)
-        send(("ry", k), img[k].at[pl.ds(0, 4), pl.ds((1 - y) * r, h)], imgin[k].at[pl.ds(0, 4)], "Y")
+        if h:
+            imgin[k][4] = jnp.zeros((h, BY, NZ), F32)
+            send(("ry", k), img[k].at[pl.ds(0, 4), pl.ds((1 - y) * r, h)], imgin[k].at[pl.ds(0, 4)], "Y")
 
     def place(first_block, storage):
         block = block_of[storage] - first_block
@@ -295,13 +341,15 @@
 
     def reduce_sibling(k):
         first, size, h, r = shape_of(k)
-        arrive(("ry", k), imgin[k].at[pl.ds(0, 4)])
+        if h:
+            arrive(("ry", k), imgin[k].at[pl.ds(0, 4)])
         for to, core in ((sibout[k], 1 - c), (acc[k], c)):
             def body(slot, carry, to=to, core=core):
                 storage = 2 * slot + core
                 to[slot] = img[k][place(my_first, storage), pl.ds(y * h, r)]
-                inner = pl.ds(y * (r - h), h)
-                to[slot, inner] = to[slot, inner] + imgin[k][place(their_first, storage)]
+                if h:
+                    inner = pl.ds(y * (r - h), h)
+                    to[slot, inner] = to[slot, inner] + imgin[k][place(their_first, storage)]
                 return carry
 
             lax.fori_loop(0, 8, body, 0)
@@ -316,27 +364,37 @@
             return carry
 
         lax.fori_loop(0, 8, body, 0)
-        send(("rd", k), acc[k].at[pl.ds(2 * column(D, way), 2)], xin[k].at[0], "B")
-        send(("ra", k), acc[k].at[pl.ds(2 * column(A, way), 2)], xin[k].at[1], "A")
-
-    def reduce_forward(k):
-        arrive(("rd", k), xin[k].at[0])
-        to_b = pl.ds(2 * column(B, way), 2)
-        acc[k][to_b] = acc[k][to_b] + xin[k][0]
-        send(("rb", k), acc[k].at[to_b], xin[k].at[2], "B")
+        for i, row in enumerate((1 - y, y)):
+            send(("rd", i, k), acc[k].at[2 * column(D, way) + row], xin[k].at[i], "B")
+            send(("ra", i, k), acc[k].at[2 * column(A, way) + row], xin[k].at[2 + i], "A")
+
+    def reduce_forward(k, i, row):
+        arrive(("rd", i, k), xin[k].at[i])
+        to_b = 2 * column(B, way) + row
+        acc[k][to_b] = acc[k][to_b] + xin[k][i]
+        send(("rb", i, k), acc[k].at[to_b], xin[k].at[4 + i], "B")
+
+    def reduce_theirs(k):
+        reduce_forward(k, 0, 1 - y)
+
+    def reduce_ours(k):
+        reduce_forward(k, 1, y)
+
+    def collected(k, i, row):
+        arrive(("ra", i, k), xin[k].at[2 + i])
+        arrive(("rb", i, k), xin[k].at[4 + i])
+        return acc[k][2 * x + row] + xin[k][2 + i] + xin[k][4 + i]
 
     def reduce_y(k):
-        arrive(("ra", k), xin[k].at[1])
-        arrive(("rb", k), xin[k].at[2])
-        mine = pl.ds(2 * x, 2)
-        acc[k][mine] = acc[k][mine] + xin[k][1] + xin[k][2]
+        acc[k][2 * x + 1 - y] = collected(k, 0, 1 - y)
         send(("rz", k), acc[k].at[2 * x + 1 - y], yin[k], "Y")
 
     def finish(k):
         first, size, h, r = shape_of(k)
+        if h:
+            imgout[k][...] = jnp.zeros((size, BY, NZ), F32)
+        imgout[k][pl.ds(y * h, r)] = collected(k, 1, y)
         arrive(("rz", k), yin[k])
-        imgout[k][...] = jnp.zeros((size, BY, NZ), F32)
-        imgout[k][pl.ds(y * h, r)] = acc[k][2 * x + y]
         theirs = pl.ds((1 - y) * h, r)
         imgout[k][theirs] = imgout[k][theirs] + yin[k][...]
         local(("image", k), imgout[k], image_out.at[pl.ds(first, size)])
@@ -344,79 +402,38 @@
     for k in ORDER:
         gather_y(k)
     first_halo = halo_send("h0", now.at[0, pl.ds(NX - HALO, HALO)], now.at[0, pl.ds(0, HALO)], fpad)
-
-    @pl.when(u == 0)
-    def _():
-        fpad[0:HALO] = jnp.zeros((HALO, NY, NZ), F32)
-        npad[0:HALO] = jnp.zeros((HALO, NY, NZ), F32)
-
-    @pl.when(u == 15)
-    def _():
-        fpad[HALO + NX:] = jnp.zeros((HALO, NY, NZ), F32)
-        npad[HALO + NX:] = jnp.zeros((HALO, NY, NZ), F32)
-
+    second_halo = []
     my_first = aperture[s]
     their_first = aperture[(x * 2 + 1 - y) * 2 + c]
     my_slots = slots_from(my_first)
     their_slots = slots_from(their_first)
-    matrices()
-    depth_spots()
-    gather_x(0)
-    gather_x(3)
-    for k in (1, 2, 0, 3):
-        locals_[("now", k)].wait()
-    prepare(1)
-    gather_forward(0)
-    gather_x(1)
-    prepare(2)
-    gather_sibling(0)
-    gather_forward(3)
-    gather_x(2)
-    halo_low(first_halo)
-    prepare(0)
-    gather_stage(0)
-    halo_high(first_halo)
-    prepare(3)
-    gather_sibling(3)
-    gather_forward(1)
-    gather_stage(3)
-    step_one(0)
-    gather_sibling(1)
-    gather_forward(2)
-    gather_stage(1)
-    step_one(3)
-    second_halo = halo_send("h1", npad.at[pl.ds(NX, HALO)], npad.at[pl.ds(HALO, HALO)], npad)
-    locals_["snap"].wait()
-    gather_sibling(2)
-    gather_stage(2)
-    step_one(1)
-    halo_low(second_halo)
-    step_two(0)
-    step_one(2)
-    halo_high(second_halo)
-    step_two(3)
-    reduce_sibling(0)
-    step_two(1)
-    reduce_x(0)
-    reduce_sibling(3)
-    step_two(2)
-    reduce_forward(0)
-    reduce_x(3)
-    reduce_sibling(1)
-    reduce_y(0)
-    reduce_forward(3)
-    reduce_x(1)
-    reduce_sibling(2)
-    finish(0)
-    reduce_y(3)
-    reduce_forward(1)
-    reduce_x(2)
-    finish(3)
-    reduce_y(1)
-    reduce_forward(2)
-    finish(1)
-    reduce_y(2)
-    finish(2)
+
+    def constants(k):
+        @pl.when(u == 0)
+        def _():
+            fpad[0:HALO] = jnp.zeros((HALO, NY, NZ), F32)
+            npad[0:HALO] = jnp.zeros((HALO, NY, NZ), F32)
+
+        @pl.when(u == 15)
+        def _():
+            fpad[HALO + NX:] = jnp.zeros((HALO, NY, NZ), F32)
+            npad[HALO + NX:] = jnp.zeros((HALO, NY, NZ), F32)
+
+        matrices()
+        depth_spots()
+        for j in range(len(CHUNKS)):
+            locals_[("now", j)].wait()
+
+    def edges(k):
+        second_halo.extend(halo_send("h1", npad.at[pl.ds(NX, HALO)], npad.at[pl.ds(HALO, HALO)], npad))
+
+    steps = {
+        "o": gather_own, "x": gather_x, "a": gather_a, "b": gather_b, "d": gather_d, "s": gather_stage,
+        "M": constants, "P": prepare, "1": step_one, "H": edges, "2": step_two,
+        "p": reduce_sibling, "q": reduce_x, "r": reduce_theirs, "R": reduce_ours, "t": reduce_y, "f": finish,
+    }
+    for name in SEQUENCE:
+        steps[name[0]](int(name[1:]))
 
     halo_sent(first_halo)
     halo_sent(second_halo)
@@ -438,7 +455,7 @@
     field = (NX, NY, NZ)
     padded = (NX + 2 * HALO, NY, NZ)
     block = (BY, NZ)
-    count = 16 * len(CHUNKS) + 8
+    count = 24 * len(CHUNKS) + 8
     scratch = [
         pltpu.VMEM(padded, F32), pltpu.VMEM(padded, F32),
         pltpu.VMEM(field, F32), pltpu.VMEM(field, F32), pltpu.VMEM(field, F32),
@@ -447,13 +464,13 @@
         pltpu.VMEM((2, NZ, 3 * NR), BF16),
         per_chunk(lambda n, h, r: (n, NY, NZ)),
         per_chunk(lambda n, h, r: (NB, r) + block),
-        per_chunk(lambda n, h, r: (h, NY, NZ)),
+        per_chunk(lambda n, h, r: (max(h, 1), NY, NZ)),
         per_chunk(lambda n, h, r: (5, n) + block),
-        per_chunk(lambda n, h, r: (5, h) + block),
+        per_chunk(lambda n, h, r: (5, max(h, 1)) + block),
         per_chunk(lambda n, h, r: (8, r) + block),
         per_chunk(lambda n, h, r: (8, r) + block),
         per_chunk(lambda n, h, r: (8, r) + block),
-        per_chunk(lambda n, h, r: (3, 2, r) + block),
+        per_chunk(lambda n, h, r: (6, r) + block),
         per_chunk(lambda n, h, r: (r,) + block),
         per_chunk(lambda n, h, r: (n,) + block),
         pltpu.SemaphoreType.DMA((count,)),

time: 110 us -> 86.1 us (0.78)
  the two profiles are of different devices: /device:TPU:32 before, /device:TPU:1 now
where the time goes in v2:
time: 86.1 us; the launch traced here: 85.5 us
  Pallas kernels  79.4 us (92%)
  local copies, waits for them, and re-layouts  5.47 us (6%)
    pallas_call x1, Pallas kernels, local(): pl.pallas_call(kernel, out_shape=(jax.ShapeDtypeStruct(field_now.shape, F...  79.4 us
    unnamed x7, local copies, waits for them, and re-layouts  5.47 us

profile of v2, /device:TPU:1, one launch (start us, length us, event | category | flops | bytes accessed | tf_op | source)
XLA Modules:
  0.0 85.5 jit_solution(6725320426384748255)
XLA Ops:
  0.6 79.4 %shard_map.103 = (f32[1,32,64,256]{3,2,1,0:T(8,128)}, f32[1,32,64,256]{3,2,1,0:T(8,128)}, f32[32,16,256]{2,1,0:T(8,128)}) custom-call(f32[1,32,64,256]{3,2,1,0:T(8,128)} %before.1, f32[1,32,64,256]{3,2,1,0:T(8,128)} %now.1, bf16[1,2,32,64,256]{4,3,2,1,0:T(8,128)(2,1)} %snapshots.1, f32[1,1,2,128]{3,2,1,0:T(2,128)} %traces.1, s32[1,1,128]{2,1,0:T(1,128)} %receivers.1, ...), custom_call_target="tpu_custom_call" | custom-call | tf_op jit(solution)/shard_map/pallas_call | solution.py:480
  80.1 0.0 copy-start
  80.1 3.3 %copy.14 = f32[1,32,64,256]{3,2,1,0:T(8,128)} copy(f32[1,32,64,256]{3,2,1,0:T(8,128)} %get-tuple-element.6) | data formatting | bytes 4194304
  83.3 0.0 copy-done
  83.3 0.0 copy-start.1
  83.3 1.3 %copy.15 = f32[1,32,64,256]{3,2,1,0:T(8,128)} copy(f32[1,32,64,256]{3,2,1,0:T(8,128)S(1)} %copy-done) | data formatting | bytes 4194304
  84.7 0.1 copy-done.1
  84.7 0.8 copy.16
Async XLA Ops:
  80.1 3.3 %copy-start = (f32[1,32,64,256]{3,2,1,0:T(8,128)S(1)}, f32[1,32,64,256]{3,2,1,0:T(8,128)}, u32[]{:S(2)}) copy-start(f32[1,32,64,256]{3,2,1,0:T(8,128)} %get-tuple-element.7) | copy-start | bytes 6291460
  83.3 1.4 %copy-start.1 = (f32[32,16,256]{2,1,0:T(8,128)S(1)}, f32[32,16,256]{2,1,0:T(8,128)}, u32[]{:S(2)}) copy-start(f32[32,16,256]{2,1,0:T(8,128)} %get-tuple-element.8) | copy-start | bytes 1572868

commit v3 on v2

--- a/solution.py
+++ b/solution.py
@@ -22,15 +22,15 @@
 ORDER = (0, 7, 1, 2, 3, 4, 5, 6)
 LOADS = tuple(range(1, len(CHUNKS) - 1)) + (0, len(CHUNKS) - 1)
 SEQUENCE = (
-    "o4", "o1", "o0", "o2", "x0", "o7", "x7", "M0", "P4", "x1", "x4", "b0", "a0", "o5",
-    "x5", "b1", "P6", "a7", "a4", "P5", "P2", "x2", "b7", "a1", "o6", "x6", "d0", "b4",
-    "a5", "d7", "s0", "d4", "P7", "o3", "x3", "s4", "d1", "P0", "a2", "b5", "b2", "s7",
-    "17", "b6", "10", "H0", "P1", "s1", "a6", "d5", "a3", "b3", "s5", "d2", "s2", "d6",
-    "P3", "d3", "14", "s3", "s6", "16", "15", "26", "p6", "11", "20", "27", "p7", "25",
-    "12", "q6", "13", "23", "q7", "24", "r6", "p0", "22", "p5", "21", "q0", "q5", "p3",
-    "q3", "t6", "p4", "r0", "r7", "r5", "p2", "r3", "q4", "R5", "q2", "p1", "q1", "t3",
-    "t0", "t7", "r2", "R3", "r4", "t5", "R0", "r1", "R1", "R6", "t2", "R7", "R2", "t4",
-    "R4", "t1", "f3", "f5", "f7", "f0", "f6", "f4", "f2", "f1",
+    "o4", "o1", "o0", "o2", "x0", "o7", "x7", "Z0", "M0", "P4", "x1", "x4", "b0", "a0",
+    "o5", "x5", "b1", "P6", "a7", "a4", "P5", "P2", "x2", "b7", "a1", "o6", "x6", "d0",
+    "b4", "a5", "d7", "s0", "d4", "P7", "o3", "x3", "s4", "d1", "P0", "a2", "b5", "b2",
+    "s7", "17", "b6", "10", "H0", "P1", "s1", "a6", "d5", "a3", "b3", "s5", "d2", "s2",
+    "d6", "P3", "d3", "14", "s3", "s6", "16", "15", "26", "p6", "11", "20", "27", "p7",
+    "25", "12", "q6", "13", "23", "q7", "24", "r6", "p0", "22", "p5", "21", "q0", "q5",
+    "p3", "q3", "t6", "p4", "r0", "r7", "r5", "p2", "r3", "q4", "R5", "q2", "p1", "q1",
+    "t3", "t0", "t7", "r2", "R3", "r4", "t5", "R0", "r1", "R1", "R6", "t2", "R7", "R2",
+    "t4", "R4", "t1", "f3", "f5", "f7", "f0", "f6", "f4", "f2", "f1",
 )
 OWN, A, B, D = range(4)
 
@@ -53,11 +53,11 @@
     return high.astype(BF16), low.astype(BF16)
 
 
-def kernel(before, now, snapshots, traces, receivers, courant, aperture, block_of,
+def kernel(before, now, snapshots, traces_in, receivers_in, courant, aperture_in, block_of_in,
            prior_out, final_out, image_out,
-           fpad, npad, base, lap, last, snap, wz, wy, spots,
+           traces, receivers, aperture, block_of, fpad, npad, base, lap, last, snap, wz, wy, spots,
            speed, gath, stage, img, imgin, sibout, sibin, acc, xin, yin, imgout,
-           send_sems, recv_sems, local_sems):
+           send_sems, recv_sems, local_sems, inside, inside_sub):
     s = lax.axis_index("shot")
     u = lax.axis_index("sub")
     c = lax.rem(s, 2)
@@ -80,8 +80,19 @@
         "S-": {"shot": s, "sub": lax.rem(u + 15, 16)},
     }
     barrier = pltpu.get_barrier_semaphore()
-    for name in dev:
-        pl.semaphore_signal(barrier, inc=1, device_id=dev[name], device_id_type=MESH)
+
+    def tell(semaphore, name):
+        pl.semaphore_signal(semaphore, inc=1, device_id=dev[name], device_id_type=MESH)
+
+    @pl.when(c == 0)
+    def _():
+        for name in "ABY":
+            tell(barrier, name)
+
+    @pl.when(c == 1)
+    def _():
+        tell(barrier, "C")
+
     first_two = [int(name[1:]) for name in SEQUENCE if name[0] == "2"][0]
     ids = {}
     sent = []
@@ -124,8 +135,24 @@
         first, size, h, r = shape_of(k)
         local(("before", k), before.at[0, pl.ds(first, size)], base.at[pl.ds(first, size)])
     local("snap", snapshots.at[0], snap)
-
-    pl.semaphore_wait(barrier, len(dev))
+    for name, src, dst in (("traces", traces_in, traces), ("receivers", receivers_in, receivers),
+                           ("aperture", aperture_in, aperture), ("block_of", block_of_in, block_of)):
+        local(name, src, dst)
+
+    @pl.when(c == 0)
+    def _():
+        pl.semaphore_wait(barrier, 4)
+        for name in "ABY":
+            tell(inside, name)
+        pl.semaphore_wait(inside, 3)
+        tell(inside, "C")
+
+    @pl.when(c == 1)
+    def _():
+        pl.semaphore_wait(inside, 1)
+        tell(barrier, "S+")
+        tell(barrier, "S-")
+
 
     def halo_send(name, up_src, down_src, pad):
         up = copy_of(name + "up", up_src, pad.at[pl.ds(0, HALO)], "S+")
@@ -401,8 +428,23 @@
 
     for k in ORDER:
         gather_y(k)
-    first_halo = halo_send("h0", now.at[0, pl.ds(NX - HALO, HALO)], now.at[0, pl.ds(0, HALO)], fpad)
+    first_halo = []
     second_halo = []
+
+    def first_edges(k):
+        @pl.when(c == 1)
+        def _():
+            pl.semaphore_wait(barrier, 2)
+            tell(inside_sub, "C")
+
+        @pl.when(c == 0)
+        def _():
+            pl.semaphore_wait(inside_sub, 1)
+
+        first_halo.extend(halo_send("h0", now.at[0, pl.ds(NX - HALO, HALO)], now.at[0, pl.ds(0, HALO)], fpad))
+
+    for name in ("traces", "receivers", "aperture", "block_of"):
+        locals_[name].wait()
     my_first = aperture[s]
     their_first = aperture[(x * 2 + 1 - y) * 2 + c]
     my_slots = slots_from(my_first)
@@ -429,7 +471,7 @@
 
     steps = {
         "o": gather_own, "x": gather_x, "a": gather_a, "b": gather_b, "d": gather_d, "s": gather_stage,
-        "M": constants, "P": prepare, "1": step_one, "H": edges, "2": step_two,
+        "Z": first_edges, "M": constants, "P": prepare, "1": step_one, "H": edges, "2": step_two,
         "p": reduce_sibling, "q": reduce_x, "r": reduce_theirs, "R": reduce_ours, "t": reduce_y, "f": finish,
     }
     for name in SEQUENCE:
@@ -446,8 +488,6 @@
 
 def local(field_before, field_now, snapshots, traces, receivers, courant, aperture, block_of):
     anywhere = pl.BlockSpec(memory_space=pl.ANY)
-    vector = pl.BlockSpec(memory_space=pltpu.VMEM)
-    scalar = pl.BlockSpec(memory_space=pltpu.SMEM)
 
     def per_chunk(dims):
         return [pltpu.VMEM(dims(size, h, size - h), F32) for first, size, h in CHUNKS]
@@ -457,6 +497,8 @@
     block = (BY, NZ)
     count = 24 * len(CHUNKS) + 8
     scratch = [
+        pltpu.VMEM(traces.shape, F32), pltpu.VMEM(receivers.shape, jnp.int32),
+        pltpu.SMEM(aperture.shape, jnp.int32), pltpu.SMEM(block_of.shape, jnp.int32),
         pltpu.VMEM(padded, F32), pltpu.VMEM(padded, F32),
         pltpu.VMEM(field, F32), pltpu.VMEM(field, F32), pltpu.VMEM(field, F32),
         pltpu.VMEM((2,) + field, BF16),
@@ -476,6 +518,8 @@
         pltpu.SemaphoreType.DMA((count,)),
         pltpu.SemaphoreType.DMA((count,)),
         pltpu.SemaphoreType.DMA((8 * len(CHUNKS),)),
+        pltpu.SemaphoreType.REGULAR,
+        pltpu.SemaphoreType.REGULAR,
     ]
     return pl.pallas_call(
         kernel,
@@ -484,7 +528,7 @@
             jax.ShapeDtypeStruct(field_now.shape, F32),
             jax.ShapeDtypeStruct(courant.shape, F32),
         ),
-        in_specs=[anywhere, anywhere, anywhere, vector, vector, anywhere, scalar, scalar],
+        in_specs=[pl.BlockSpec(memory_space=pltpu.HBM)] * 8,
         out_specs=(anywhere, anywhere, anywhere),
         scratch_shapes=scratch,
         compiler_params=pltpu.CompilerParams(

time: 86.1 us -> 82.1 us (0.954)
  Pallas kernels: 79.4 us -> 75.8 us
    pallas_call x1, Pallas kernels: 79.4 us -> 75.8 us  [local(): pl.pallas_call(kernel, out_shape=(jax.ShapeDtypeStruct(field_now.shape, F...]
where the time goes in v3:
time: 82.1 us; the launch traced here: 81.9 us
  Pallas kernels  75.8 us (92%)
  local copies, waits for them, and re-layouts  5.47 us (7%)
    pallas_call x1, Pallas kernels, local(): pl.pallas_call(kernel, out_shape=(jax.ShapeDtypeStruct(field_now.shape, F...  75.8 us
    unnamed x7, local copies, waits for them, and re-layouts  5.47 us

profile of v3, /device:TPU:1, one launch (start us, length us, event | category | flops | bytes accessed | tf_op | source)
XLA Modules:
  0.0 81.9 jit_solution(10530548153679892854)
XLA Ops:
  0.6 75.8 %shard_map.103 = (f32[1,32,64,256]{3,2,1,0:T(8,128)}, f32[1,32,64,256]{3,2,1,0:T(8,128)}, f32[32,16,256]{2,1,0:T(8,128)}) custom-call(f32[1,32,64,256]{3,2,1,0:T(8,128)} %before.1, f32[1,32,64,256]{3,2,1,0:T(8,128)} %now.1, bf16[1,2,32,64,256]{4,3,2,1,0:T(8,128)(2,1)} %snapshots.1, f32[1,1,2,128]{3,2,1,0:T(2,128)} %traces_in.1, s32[1,1,128]{2,1,0:T(1,128)} %receivers_in.1, ...), custom_call_target="tpu_custom_call" | custom-call | tf_op jit(solution)/shard_map/pallas_call | solution.py:524
  76.5 0.0 copy-start
  76.5 3.3 %copy.14 = f32[1,32,64,256]{3,2,1,0:T(8,128)} copy(f32[1,32,64,256]{3,2,1,0:T(8,128)} %get-tuple-element.6) | data formatting | bytes 4194304
  79.7 0.0 copy-done
  79.7 0.0 copy-start.1
  79.8 1.3 %copy.15 = f32[1,32,64,256]{3,2,1,0:T(8,128)} copy(f32[1,32,64,256]{3,2,1,0:T(8,128)S(1)} %copy-done) | data formatting | bytes 4194304
  81.1 0.1 copy-done.1
  81.1 0.8 copy.16
Async XLA Ops:
  76.5 3.3 %copy-start = (f32[1,32,64,256]{3,2,1,0:T(8,128)S(1)}, f32[1,32,64,256]{3,2,1,0:T(8,128)}, u32[]{:S(2)}) copy-start(f32[1,32,64,256]{3,2,1,0:T(8,128)} %get-tuple-element.7) | copy-start | bytes 6291460
  79.7 1.4 %copy-start.1 = (f32[32,16,256]{2,1,0:T(8,128)S(1)}, f32[32,16,256]{2,1,0:T(8,128)}, u32[]{:S(2)}) copy-start(f32[32,16,256]{2,1,0:T(8,128)} %get-tuple-element.8) | copy-start | bytes 1572868

commit v4 on v3

--- a/solution.py
+++ b/solution.py
@@ -18,19 +18,19 @@
 centre_weight = -205.0 / 72.0
 side_weights = (8.0 / 5.0, -1.0 / 5.0, 8.0 / 315.0, -1.0 / 560.0)
 
-CHUNKS = ((0, 4, 1), (4, 4, 2), (8, 4, 2), (12, 4, 2), (16, 4, 2), (20, 4, 1), (24, 4, 0), (28, 4, 0))
-ORDER = (0, 7, 1, 2, 3, 4, 5, 6)
+CHUNKS = ((0, 4, 2), (4, 4, 0), (8, 4, 2), (12, 4, 0), (16, 4, 1), (20, 4, 2), (24, 4, 2), (28, 4, 0))
+ORDER = (7, 0, 1, 2, 3, 4, 5, 6)
 LOADS = tuple(range(1, len(CHUNKS) - 1)) + (0, len(CHUNKS) - 1)
 SEQUENCE = (
-    "o4", "o1", "o0", "o2", "x0", "o7", "x7", "Z0", "M0", "P4", "x1", "x4", "b0", "a0",
-    "o5", "x5", "b1", "P6", "a7", "a4", "P5", "P2", "x2", "b7", "a1", "o6", "x6", "d0",
-    "b4", "a5", "d7", "s0", "d4", "P7", "o3", "x3", "s4", "d1", "P0", "a2", "b5", "b2",
-    "s7", "17", "b6", "10", "H0", "P1", "s1", "a6", "d5", "a3", "b3", "s5", "d2", "s2",
-    "d6", "P3", "d3", "14", "s3", "s6", "16", "15", "26", "p6", "11", "20", "27", "p7",
-    "25", "12", "q6", "13", "23", "q7", "24", "r6", "p0", "22", "p5", "21", "q0", "q5",
-    "p3", "q3", "t6", "p4", "r0", "r7", "r5", "p2", "r3", "q4", "R5", "q2", "p1", "q1",
-    "t3", "t0", "t7", "r2", "R3", "r4", "t5", "R0", "r1", "R1", "R6", "t2", "R7", "R2",
-    "t4", "R4", "t1", "f3", "f5", "f7", "f0", "f6", "f4", "f2", "f1",
+    "o7", "o0", "M0", "o5", "o2", "x0", "x7", "Z0", "x2", "o1", "a0", "P4", "a7", "b0",
+    "a2", "P2", "o4", "x4", "b2", "d0", "o3", "s0", "o6", "x6", "x5", "d2", "b7", "x1",
+    "s2", "d7", "P0", "P7", "a4", "x3", "s7", "17", "10", "H0", "a6", "b6", "P3", "b1",
+    "b4", "a1", "d4", "b5", "a5", "a3", "12", "s4", "d6", "d1", "s6", "d5", "b3", "P1",
+    "s1", "d3", "11", "s5", "21", "p1", "14", "s3", "13", "23", "p3", "22", "P6", "q1",
+    "P5", "16", "27", "q3", "p7", "15", "26", "24", "r1", "20", "25", "r3", "q7", "p2",
+    "q2", "p6", "r7", "p4", "q6", "p0", "t3", "r2", "q4", "q0", "p5", "t7", "t1", "r4",
+    "q5", "r0", "t2", "r6", "R3", "r5", "R0", "t4", "R4", "R1", "R6", "t0", "t6", "R2",
+    "R7", "t5", "R5", "f1", "f3", "f2", "f6", "f4", "f0", "f7", "f5",
 )
 OWN, A, B, D = range(4)
 
@@ -484,6 +484,25 @@
     for name in locals_:
         if name[0] in ("prior", "final", "image"):
             locals_[name].wait()
+
+
+def hand_on(prior, final, image, prior_out, final_out, image_out, prior_held, final_held, image_held,
+            in_sems, out_sems):
+    pieces = []
+    for piece in range(4):
+        rows = pl.ds(8 * piece, 8)
+        pieces.append((prior.at[0, rows], prior_held.at[rows], prior_out.at[0, rows]))
+        pieces.append((final.at[0, rows], final_held.at[rows], final_out.at[0, rows]))
+    pieces.append((image, image_held, image_out))
+    loads = [pltpu.make_async_copy(src, held, in_sems.at[i]) for i, (src, held, dst) in enumerate(pieces)]
+    stores = [pltpu.make_async_copy(held, dst, out_sems.at[i]) for i, (src, held, dst) in enumerate(pieces)]
+    for load in loads:
+        load.start()
+    for load, store in zip(loads, stores):
+        load.wait()
+        store.start()
+    for store in stores:
+        store.wait()
 
 
 def local(field_before, field_now, snapshots, traces, receivers, courant, aperture, block_of):
@@ -521,7 +540,7 @@
         pltpu.SemaphoreType.REGULAR,
         pltpu.SemaphoreType.REGULAR,
     ]
-    return pl.pallas_call(
+    results = pl.pallas_call(
         kernel,
         out_shape=(
             jax.ShapeDtypeStruct(field_now.shape, F32),
@@ -534,6 +553,18 @@
         compiler_params=pltpu.CompilerParams(
             collective_id=0, has_side_effects=True, vmem_limit_bytes=60 << 20),
     )(field_before, field_now, snapshots, traces, receivers, courant, aperture, block_of)
+    return pl.pallas_call(
+        hand_on,
+        out_shape=tuple(jax.ShapeDtypeStruct(result.shape, F32) for result in results),
+        in_specs=[pl.BlockSpec(memory_space=pltpu.HBM)] * 3,
+        out_specs=(pl.BlockSpec(memory_space=pltpu.HBM),) * 3,
+        scratch_shapes=[
+            pltpu.VMEM(results[0].shape[1:], F32), pltpu.VMEM(results[1].shape[1:], F32),
+            pltpu.VMEM(results[2].shape, F32),
+            pltpu.SemaphoreType.DMA((9,)), pltpu.SemaphoreType.DMA((9,)),
+        ],
+        compiler_params=pltpu.CompilerParams(vmem_limit_bytes=60 << 20),
+    )(*results)
 
 
 def solution(mesh):

time: 82.1 us -> 79.8 us (0.972)
  the two profiles are of different devices: /device:TPU:1 before, /device:TPU:240 now
where the time goes in v4:
time: 79.8 us; the launch traced here: 79.7 us
  Pallas kernels  79.1 us (99%)
    pallas_call x1, Pallas kernels, local(): pl.pallas_call(kernel, out_shape=(jax.ShapeDtypeStruct(field_now.shape, F...  74.9 us
    pallas_call x1, Pallas kernels, local(): pl.pallas_call(hand_on, out_shape=tuple((jax.ShapeDtypeStruct(result.shap...  4.16 us

profile of v4, /device:TPU:240, one launch (start us, length us, event | category | flops | bytes accessed | tf_op | source)
XLA Modules:
  0.0 79.7 jit_solution(13087847164965469061)
XLA Ops:
  0.6 74.9 %shard_map.103 = (f32[1,32,64,256]{3,2,1,0:T(8,128)}, f32[1,32,64,256]{3,2,1,0:T(8,128)}, f32[32,16,256]{2,1,0:T(8,128)}) custom-call(f32[1,32,64,256]{3,2,1,0:T(8,128)} %before.1, f32[1,32,64,256]{3,2,1,0:T(8,128)} %now.1, bf16[1,2,32,64,256]{4,3,2,1,0:T(8,128)(2,1)} %snapshots.1, f32[1,1,2,128]{3,2,1,0:T(2,128)} %traces_in.1, s32[1,1,128]{2,1,0:T(1,128)} %receivers_in.1, ...), custom_call_target="tpu_custom_call" | custom-call | tf_op jit(solution)/shard_map/pallas_call | solution.py:543
  75.6 4.2 %shard_map.104 = (f32[1,32,64,256]{3,2,1,0:T(8,128)}, f32[1,32,64,256]{3,2,1,0:T(8,128)}, f32[32,16,256]{2,1,0:T(8,128)}) custom-call(f32[1,32,64,256]{3,2,1,0:T(8,128)} %get-tuple-element.6.prior, f32[1,32,64,256]{3,2,1,0:T(8,128)} %get-tuple-element.7.final, f32[32,16,256]{2,1,0:T(8,128)} %get-tuple-element.8.image), custom_call_target="tpu_custom_call" | custom-call | tf_op jit(solution)/shard_map/pallas_call | solution.py:556

commit v5 on v4

--- a/solution.py
+++ b/solution.py
@@ -386,14 +386,17 @@
     def reduce_x(k):
         arrive(("rc", k), sibin[k])
 
-        def body(slot, carry):
+        def add(role, row):
+            slot = 2 * column(role, way) + row
             acc[k][slot] = acc[k][slot] + sibin[k][slot]
-            return carry
-
-        lax.fori_loop(0, 8, body, 0)
+            return acc[k].at[slot]
+
         for i, row in enumerate((1 - y, y)):
-            send(("rd", i, k), acc[k].at[2 * column(D, way) + row], xin[k].at[i], "B")
-            send(("ra", i, k), acc[k].at[2 * column(A, way) + row], xin[k].at[2 + i], "A")
+            send(("rd", i, k), add(D, row), xin[k].at[i], "B")
+            send(("ra", i, k), add(A, row), xin[k].at[2 + i], "A")
+        for role in (B, OWN):
+            for row in (1 - y, y):
+                add(role, row)
 
     def reduce_forward(k, i, row):
         arrive(("rd", i, k), xin[k].at[i])

time: 79.8 us -> 79.9 us (level)
  no operation moved by 1% of the time
where the time goes in v5:
time: 79.9 us; the launch traced here: 79.8 us
  Pallas kernels  79.1 us (99%)
    pallas_call x1, Pallas kernels, local(): pl.pallas_call(kernel, out_shape=(jax.ShapeDtypeStruct(field_now.shape, F...  75 us
    pallas_call x1, Pallas kernels, local(): pl.pallas_call(hand_on, out_shape=tuple((jax.ShapeDtypeStruct(result.shap...  4.16 us

profile of v5, /device:TPU:240, one launch (start us, length us, event | category | flops | bytes accessed | tf_op | source)
XLA Modules:
  0.0 79.8 jit_solution(10838238227325247683)
XLA Ops:
  0.6 75.0 %shard_map.103 = (f32[1,32,64,256]{3,2,1,0:T(8,128)}, f32[1,32,64,256]{3,2,1,0:T(8,128)}, f32[32,16,256]{2,1,0:T(8,128)}) custom-call(f32[1,32,64,256]{3,2,1,0:T(8,128)} %before.1, f32[1,32,64,256]{3,2,1,0:T(8,128)} %now.1, bf16[1,2,32,64,256]{4,3,2,1,0:T(8,128)(2,1)} %snapshots.1, f32[1,1,2,128]{3,2,1,0:T(2,128)} %traces_in.1, s32[1,1,128]{2,1,0:T(1,128)} %receivers_in.1, ...), custom_call_target="tpu_custom_call" | custom-call | tf_op jit(solution)/shard_map/pallas_call | solution.py:546
  75.6 4.2 %shard_map.104 = (f32[1,32,64,256]{3,2,1,0:T(8,128)}, f32[1,32,64,256]{3,2,1,0:T(8,128)}, f32[32,16,256]{2,1,0:T(8,128)}) custom-call(f32[1,32,64,256]{3,2,1,0:T(8,128)} %get-tuple-element.6.prior, f32[1,32,64,256]{3,2,1,0:T(8,128)} %get-tuple-element.7.final, f32[32,16,256]{2,1,0:T(8,128)} %get-tuple-element.8.image), custom_call_target="tpu_custom_call" | custom-call | tf_op jit(solution)/shard_map/pallas_call | solution.py:559
